TPU v7x, 128 devices: a whole 4x4x4 slice. The times are simulated.
128 devices in a mesh: day: 32 (over z, x, core), pt: 4 (over y).
Axes of the slice: x: 4, y: 4, z: 4, core: 2. Of those that a mesh axis runs over, the one named last changes fastest.
Arguments:
- points: bfloat16 [32, 64, 2048], P('day', None, 'pt'), may hold values from -0.45 to 0.45
- cells: bfloat16 [32, 64, 8192], P('day', None, 'pt'), may hold values from -0.44921875 to 0.44921875
- clone_weight: float32 [32, 64, 2048], P('day', None, 'pt'), may hold values from 0.1 to 1
- potential: float32 [32, 2048], P('day', 'pt'), may hold values from 0.2 to 5
- support_count: int32 [32], P('day'), may hold values from 512 to 2048, as said below
- cell_count: int32 [32], P('day'), may hold values from 2048 to 8192, as said below
Outputs:
- forward_message: float32 [32, 64, 2048], P('day', None, 'pt')
- backward_message: float32 [32, 64, 2048], P('day', None, 'pt')
- fit_ratio: float32 [32, 2048], P('day', 'pt')
Inputs may be any that keep to these rules, and one draw needn't show every extreme that they name: Live support points of a day are its first support_count slots; some day has all 2048 slots live and some day has 512. Observed cells of a day are its first cell_count slots; some day fills all 8192 slots and some day has 2048.
All inputs are finite; a program needn't handle non-finite values.
Results may differ from a plain program's by a relative error of at most 0.0003.
Values may be sent and summed in bfloat16 or wider, within the bound.
A program may use at most 64 MiB of HBM per device.

v0:
```python
import jax
import jax.numpy as jnp
from jax import lax
from jax.sharding import PartitionSpec as P


def with_halo(cells, sides, width):
    for axis, dim in sides:
        count = lax.axis_size(axis)
        ends = count - 1
        head = lax.slice_in_dim(cells, 0, width, axis=dim)
        tail = lax.slice_in_dim(cells, cells.shape[dim] - width, cells.shape[dim], axis=dim)
        cells = jnp.concatenate(
            [
                lax.ppermute(tail, axis, [(i, (i + 1) % count) for i in range(ends)]),
                cells,
                lax.ppermute(head, axis, [((i + 1) % count, i) for i in range(ends)]),
            ],
            axis=dim,
        )
    return cells


def shifted(block, axis, distance):
    devices = range(lax.axis_size(axis))
    route = [(i - distance, i) for i in devices if i - distance in devices]
    return lax.ppermute(block, axis, route)


def norm_of(coords):
    wide = coords.astype(jnp.float32)
    return jnp.sum(wide * wide, axis=0)


def squared_dist(left_pts, left_norm, right_pts, right_norm):
    inner = lax.dot_general(
        left_pts, right_pts, (((0,), (0,)), ((), ())), preferred_element_type=jnp.float32
    )
    return left_norm[:, None] + right_norm[None, :] - 2.0 * inner


def shards(points, cells, clone_weight, potential, support_count, cell_count):
    pt_rank = lax.axis_index("pt")
    day_index = lax.axis_index("day")
    day_count = lax.axis_size("day")
    full_pts, full_clone, full_pot = (
        lax.all_gather(points.astype(jnp.float32), "pt", axis=2, tiled=True).astype(points.dtype),
        lax.all_gather(clone_weight, "pt", axis=2, tiled=True),
        lax.all_gather(potential, "pt", axis=1, tiled=True),
    )
    beside_all = with_halo(full_pts, (("day", 0),), 1)
    before_day = beside_all[0]
    after_day = beside_all[2]
    own_pts = points[0]
    per_device = own_pts.shape[1]
    support_total = full_pts.shape[2]
    clones = clone_weight.shape[1]
    weight = full_clone[0] * full_pot
    live_total = support_count[0].astype(jnp.float32)
    live_all = (jnp.arange(support_total, dtype=jnp.int32) < support_count[0]).astype(jnp.float32)
    live_own = lax.dynamic_slice_in_dim(live_all, pt_rank * per_device, per_device)
    own_norm = norm_of(own_pts)
    before_norm = norm_of(before_day)
    after_norm = norm_of(after_day)
    row_span = 512
    span_count = support_total // row_span

    def kernel_rows(source_pts, source_norm, block_index):
        offset = block_index * row_span
        source_rows = lax.dynamic_slice_in_dim(source_pts, offset, row_span, 1)
        norm_rows = lax.dynamic_slice_in_dim(source_norm, offset, row_span, 0)
        return jnp.exp(-squared_dist(source_rows, norm_rows, own_pts, own_norm)).astype(
            jnp.bfloat16
        )

    def contract(sent_rows, source_pts, source_norm):

        def add_rows(block_index, result):
            sent_part = lax.dynamic_slice_in_dim(sent_rows, block_index * row_span, row_span, 1)
            return result + jnp.dot(
                sent_part,
                kernel_rows(source_pts, source_norm, block_index),
                preferred_element_type=jnp.float32,
            )

        return lax.fori_loop(
            0, span_count, add_rows, jnp.zeros((sent_rows.shape[0], per_device), jnp.float32)
        )

    block_count = 4
    block_rows = clones // block_count
    steps_total = day_count + block_count - 1
    empty_rows = jnp.zeros((block_rows, per_device), jnp.float32)
    seed_rows = jnp.broadcast_to(live_own[None, :], (block_rows, per_device))

    def settle(piece_rows, full_rows, valid):
        column_sums = jnp.sum(full_rows * live_all[None, :], axis=1, keepdims=True)
        column_sums = jnp.where(valid, column_sums, 1.0)
        own_part = piece_rows * live_own[None, :] * live_total / column_sums
        whole_part = full_rows * live_all[None, :] * live_total / column_sums
        return (own_part, whole_part)

    def one_step(step_index, carried):
        forward_in, backward_in, forward_out, backward_out = carried
        forward_at = step_index - day_index
        forward_ok = (forward_at >= 0) & (forward_at < block_count)
        forward_block = jnp.clip(forward_at, 0, block_count - 1)
        backward_at = step_index - (day_count - 1 - day_index)
        backward_ok = (backward_at >= 0) & (backward_at < block_count)
        backward_block = jnp.clip(backward_at, 0, block_count - 1)
        forward_got = lax.cond(
            forward_ok & (day_index > 0),
            lambda: contract(forward_in, before_day, before_norm),
            lambda: empty_rows,
        )
        forward_piece = jnp.where(day_index == 0, seed_rows, forward_got)
        backward_got = lax.cond(
            backward_ok & (day_index < day_count - 1),
            lambda: contract(backward_in, after_day, after_norm),
            lambda: empty_rows,
        )
        backward_piece = jnp.where(day_index == day_count - 1, seed_rows, backward_got)
        forward_full, backward_full = (
            lax.all_gather(forward_piece, "pt", axis=1, tiled=True),
            lax.all_gather(backward_piece, "pt", axis=1, tiled=True),
        )
        forward_own, forward_all = settle(forward_piece, forward_full, forward_ok)
        backward_own, backward_all = settle(backward_piece, backward_full, backward_ok)
        forward_out = jnp.where(
            forward_ok,
            lax.dynamic_update_slice_in_dim(
                forward_out, forward_own, forward_block * block_rows, 0
            ),
            forward_out,
        )
        backward_out = jnp.where(
            backward_ok,
            lax.dynamic_update_slice_in_dim(
                backward_out, backward_own, backward_block * block_rows, 0
            ),
            backward_out,
        )
        forward_sent = (
            forward_all
            * lax.dynamic_slice_in_dim(weight, forward_block * block_rows, block_rows, 0)
        ).astype(jnp.bfloat16)
        backward_sent = (
            backward_all
            * lax.dynamic_slice_in_dim(weight, backward_block * block_rows, block_rows, 0)
        ).astype(jnp.bfloat16)
        forward_in = shifted(forward_sent, "day", 1)
        backward_in = shifted(backward_sent, "day", -1)
        return (forward_in, backward_in, forward_out, backward_out)

    start_in = jnp.zeros((block_rows, support_total), jnp.bfloat16)
    start_out = jnp.zeros((clones, per_device), jnp.float32)
    carried = lax.fori_loop(0, steps_total, one_step, (start_in, start_in, start_out, start_out))
    forward_out = carried[2]
    backward_out = carried[3]
    mass_own = (
        live_own * potential[0] * jnp.sum(forward_out * clone_weight[0] * backward_out, axis=0)
    )
    cell_total = cell_count[0]
    cell_total_f = cell_total.astype(jnp.float32)
    all_cells = lax.all_gather(cells, "pt", axis=2, tiled=True)[0]
    cell_slots = all_cells.shape[1]
    cell_norm = norm_of(all_cells)
    fit_span = 512
    fit_blocks = cell_slots // fit_span

    def fit_columns(block_index):
        offset = block_index * fit_span
        chosen = lax.dynamic_slice_in_dim(all_cells, offset, fit_span, 1)
        chosen_norm = lax.dynamic_slice_in_dim(cell_norm, offset, fit_span, 0)
        return jnp.exp(-squared_dist(own_pts, own_norm, chosen, chosen_norm))

    def density_part(block_index):
        return jnp.dot(mass_own, fit_columns(block_index), precision=lax.Precision.HIGHEST)

    partial_density = lax.map(density_part, jnp.arange(fit_blocks)).reshape(cell_slots)
    column_sums, mass_total = lax.psum((partial_density, jnp.sum(mass_own)), "pt")
    density = column_sums / mass_total
    cell_live = (jnp.arange(cell_slots, dtype=jnp.int32) < cell_total).astype(jnp.float32)
    inverse = cell_live / density

    def ratio_part(block_index, running):
        chosen_inverse = lax.dynamic_slice_in_dim(inverse, block_index * fit_span, fit_span, 0)
        return running + jnp.dot(
            fit_columns(block_index), chosen_inverse, precision=lax.Precision.HIGHEST
        )

    summed = lax.fori_loop(0, fit_blocks, ratio_part, jnp.zeros((per_device,), jnp.float32))
    fit_rows_out = live_own / cell_total_f * summed
    return (forward_out[None], backward_out[None], fit_rows_out[None])


def solution(mesh):
    in_specs = (
        P("day", None, "pt"),
        P("day", None, "pt"),
        P("day", None, "pt"),
        P("day", "pt"),
        P("day"),
        P("day"),
    )
    out_specs = (P("day", None, "pt"), P("day", None, "pt"), P("day", "pt"))
    return jax.shard_map(shards, mesh=mesh, in_specs=in_specs, out_specs=out_specs, check_vma=False)
```

profile of v0, /device:TPU:0, one launch (start us, length us, event | category | flops | bytes accessed | tf_op | source)
XLA Modules:
  0.0 1607.6 jit_solution(1951104666775304493)
XLA Ops:
  7.2 13.1 all_gather.28
  24.8 13.6 all_gather.29
  50.4 1437.5 %while.76 = (s32[]{:T(128)}, bf16[16,2048]{1,0:T(8,128)(2,1)S(1)}, bf16[16,2048]{1,0:T(8,128)(2,1)S(1)}, f32[64,512]{1,0:T(8,128)S(1)}, f32[64,512]{1,0:T(8,128)...) while((s32[]{:T(128)}, bf16[16,2048]{1,0:T(8,128)(2,1)S(1)}, ...), condition=%wide.region_14.15_spmd.clone.clone, body=%wide.region_3.14_spmd.clone.clone.sunk | while | flops 87085088 | bytes 2573997 | solution.py:157
  85.6 12.0 all_gather.38
  121.1 12.0 all_gather.38
  161.5 12.0 all_gather.38
  243.1 12.0 all_gather.38
  283.9 12.0 all_gather.38
  318.3 12.0 all_gather.38
  352.6 12.0 all_gather.38
  597.5 13.3 collective-permute-done.1
  822.8 18.5 %collective-permute-done.1 = bf16[16,2048]{1,0:T(8,128)(2,1)S(1)} collective-permute-done((bf16[16,2048]{1,0:T(8,128)(2,1)S(1)}, bf16[16,2048]{1,0:T(8,128)(2,1)S(1)}, u32[]{:S(2)}, u32[]{:S(2)}) %collective-permute-start.1) | collective-permute-done | bytes 65568 | tf_op jit(solution)/shard_map/while/body/eval_jaxpr/ppermute | solution.py:27
  871.0 13.2 collective-permute-done.1
  913.8 17.7 %collective-permute-done.1 = bf16[16,2048]{1,0:T(8,128)(2,1)S(1)} collective-permute-done((bf16[16,2048]{1,0:T(8,128)(2,1)S(1)}, bf16[16,2048]{1,0:T(8,128)(2,1)S(1)}, u32[]{:S(2)}, u32[]{:S(2)}) %collective-permute-start.1) | collective-permute-done | bytes 65568 | tf_op jit(solution)/shard_map/while/body/eval_jaxpr/ppermute | solution.py:27
  961.2 26.2 %collective-permute-done.1 = bf16[16,2048]{1,0:T(8,128)(2,1)S(1)} collective-permute-done((bf16[16,2048]{1,0:T(8,128)(2,1)S(1)}, bf16[16,2048]{1,0:T(8,128)(2,1)S(1)}, u32[]{:S(2)}, u32[]{:S(2)}) %collective-permute-start.1) | collective-permute-done | bytes 65568 | tf_op jit(solution)/shard_map/while/body/eval_jaxpr/ppermute | solution.py:27
  1016.9 19.6 %collective-permute-done.1 = bf16[16,2048]{1,0:T(8,128)(2,1)S(1)} collective-permute-done((bf16[16,2048]{1,0:T(8,128)(2,1)S(1)}, bf16[16,2048]{1,0:T(8,128)(2,1)S(1)}, u32[]{:S(2)}, u32[]{:S(2)}) %collective-permute-start.1) | collective-permute-done | bytes 65568 | tf_op jit(solution)/shard_map/while/body/eval_jaxpr/ppermute | solution.py:27
  1066.2 26.1 %collective-permute-done.1 = bf16[16,2048]{1,0:T(8,128)(2,1)S(1)} collective-permute-done((bf16[16,2048]{1,0:T(8,128)(2,1)S(1)}, bf16[16,2048]{1,0:T(8,128)(2,1)S(1)}, u32[]{:S(2)}, u32[]{:S(2)}) %collective-permute-start.1) | collective-permute-done | bytes 65568 | tf_op jit(solution)/shard_map/while/body/eval_jaxpr/ppermute | solution.py:27
  1121.9 19.9 %collective-permute-done.1 = bf16[16,2048]{1,0:T(8,128)(2,1)S(1)} collective-permute-done((bf16[16,2048]{1,0:T(8,128)(2,1)S(1)}, bf16[16,2048]{1,0:T(8,128)(2,1)S(1)}, u32[]{:S(2)}, u32[]{:S(2)}) %collective-permute-start.1) | collective-permute-done | bytes 65568 | tf_op jit(solution)/shard_map/while/body/eval_jaxpr/ppermute | solution.py:27
  1171.4 19.7 %collective-permute-done.1 = bf16[16,2048]{1,0:T(8,128)(2,1)S(1)} collective-permute-done((bf16[16,2048]{1,0:T(8,128)(2,1)S(1)}, bf16[16,2048]{1,0:T(8,128)(2,1)S(1)}, u32[]{:S(2)}, u32[]{:S(2)}) %collective-permute-start.1) | collective-permute-done | bytes 65568 | tf_op jit(solution)/shard_map/while/body/eval_jaxpr/ppermute | solution.py:27
  1220.8 19.8 %collective-permute-done.1 = bf16[16,2048]{1,0:T(8,128)(2,1)S(1)} collective-permute-done((bf16[16,2048]{1,0:T(8,128)(2,1)S(1)}, bf16[16,2048]{1,0:T(8,128)(2,1)S(1)}, u32[]{:S(2)}, u32[]{:S(2)}) %collective-permute-start.1) | collective-permute-done | bytes 65568 | tf_op jit(solution)/shard_map/while/body/eval_jaxpr/ppermute | solution.py:27
  1270.1 19.7 %collective-permute-done.1 = bf16[16,2048]{1,0:T(8,128)(2,1)S(1)} collective-permute-done((bf16[16,2048]{1,0:T(8,128)(2,1)S(1)}, bf16[16,2048]{1,0:T(8,128)(2,1)S(1)}, u32[]{:S(2)}, u32[]{:S(2)}) %collective-permute-start.1) | collective-permute-done | bytes 65568 | tf_op jit(solution)/shard_map/while/body/eval_jaxpr/ppermute | solution.py:27
  1490.1 52.7 %while.74 = (s32[]{:T(128)}, f32[16,512]{1,0:T(8,128)S(1)}, f32[512]{0:T(512)S(1)}, s32[16]{0:T(128)S(1)}, f32[8192]{0:T(1024)S(1)}, /*index=5*/bf16[64,8192]{1,...) while((s32[]{:T(128)}, f32[16,512]{1,0:T(8,128)S(1)}, ...), condition=%wide.region_20.21_spmd, body=%wide.region_19.20_spmd.sunk | while | flops 37748740 | bytes 2244795 | solution.py:180
  1542.9 18.0 %all-reduce = (f32[8192]{0:T(1024)S(1)}, f32[]{:T(128)}) all-reduce(f32[8192]{0:T(1024)S(1)} %bitcast.96, f32[]{:T(128)} %get-tuple-element.1099), channel_id=1, replica_groups=mesh['day'=32,'pt'=4] {'pt'}, use_global_device_ids=true, to_apply=%region_21.22 | all-reduce | flops 8193 | bytes 65544 | tf_op jit(solution)/shard_map/psum | solution.py:181
  1561.6 38.6 %while.75 = (s32[]{:T(128)}, f32[512]{0:T(512)S(1)}, f32[512]{0:T(512)S(1)}, f32[8192]{0:T(1024)S(1)}, bf16[64,8192]{1,0:T(8,128)(2,1)}, /*index=5*/bf16[64,512]...) while((s32[]{:T(128)}, f32[512]{0:T(512)S(1)}, ...), condition=%wide.region_23.24_spmd.clone, body=%wide.region_22.23_spmd.clone.sunk | while | flops 37749764 | bytes 2250929 | solution.py:192
  (774 shorter events, 1333.4 us)
Async XLA Ops:
  7.2 1481.4 %all-gather.2.cloned.1.call-start = ((), (), s32[]{:S(2)}) async-start(), calls=%async_computation | async-start | bytes 1310720 | tf_op jit(solution)/shard_map/all_gather | solution.py:165
  20.3 29.9 %collective-permute-start.3 = (bf16[1,64,2048]{2,1,0:T(8,128)(2,1)S(1)}, bf16[1,64,2048]{2,1,0:T(8,128)(2,1)S(1)}, u32[]{:S(2)}, u32[]{:S(2)}) collective-permute-start(bf16[1,64,2048]{2,1,0:T(8,128)(2,1)S(1)} %all_gather.28), channel_id=1, source_target_pairs={{4,0},{8,4},{12,8},{16,12},{20,16},{24,20},{28,24},{32,28},{36,32}... | collective-permute-start | bytes 786440 | tf_op jit(solution)/shard_map/ppermute | solution.py:17
  21.7 28.6 %collective-permute-start.2 = (bf16[1,64,2048]{2,1,0:T(8,128)(2,1)S(1)}, bf16[1,64,2048]{2,1,0:T(8,128)(2,1)S(1)}, u32[]{:S(2)}, u32[]{:S(2)}) collective-permute-start(bf16[1,64,2048]{2,1,0:T(8,128)(2,1)S(1)} %all_gather.28), channel_id=1, source_target_pairs={{0,4},{4,8},{8,12},{12,16},{16,20},{20,24},{24,28},{28,32},{32,36}... | collective-permute-start | bytes 786440 | tf_op jit(solution)/shard_map/ppermute | solution.py:15
  151.2 8.3 collective-permute-start.1
  191.9 8.4 collective-permute-start.1
  232.7 8.4 collective-permute-start.1
  269.3 12.6 collective-permute-start.1
  378.9 8.3 collective-permute-start.1
  484.1 10.3 collective-permute-start.1
  557.0 10.9 collective-permute-start.1
  596.1 14.7 collective-permute-start.1
  639.0 8.3 collective-permute-start.1
  784.9 8.3 collective-permute-start.1
  821.4 19.9 %collective-permute-start.1 = (bf16[16,2048]{1,0:T(8,128)(2,1)S(1)}, bf16[16,2048]{1,0:T(8,128)(2,1)S(1)}, u32[]{:S(2)}, u32[]{:S(2)}) collective-permute-start(bf16[16,2048]{1,0:T(8,128)(2,1)S(1)} %get-tuple-element.1417), channel_id=1, source_target_pairs={{4,0},{8,4},{12,8},{16,12},{20,16},{24,20},{28,24},{32,28},{36,32}... | collective-permute-start | bytes 196616 | tf_op jit(solution)/shard_map/while/body/eval_jaxpr/ppermute | solution.py:27
  869.6 14.6 collective-permute-start.1
  912.4 19.1 %collective-permute-start.1 = (bf16[16,2048]{1,0:T(8,128)(2,1)S(1)}, bf16[16,2048]{1,0:T(8,128)(2,1)S(1)}, u32[]{:S(2)}, u32[]{:S(2)}) collective-permute-start(bf16[16,2048]{1,0:T(8,128)(2,1)S(1)} %get-tuple-element.1417), channel_id=1, source_target_pairs={{4,0},{8,4},{12,8},{16,12},{20,16},{24,20},{28,24},{32,28},{36,32}... | collective-permute-start | bytes 196616 | tf_op jit(solution)/shard_map/while/body/eval_jaxpr/ppermute | solution.py:27
  959.8 27.6 %collective-permute-start.1 = (bf16[16,2048]{1,0:T(8,128)(2,1)S(1)}, bf16[16,2048]{1,0:T(8,128)(2,1)S(1)}, u32[]{:S(2)}, u32[]{:S(2)}) collective-permute-start(bf16[16,2048]{1,0:T(8,128)(2,1)S(1)} %get-tuple-element.1417), channel_id=1, source_target_pairs={{4,0},{8,4},{12,8},{16,12},{20,16},{24,20},{28,24},{32,28},{36,32}... | collective-permute-start | bytes 196616 | tf_op jit(solution)/shard_map/while/body/eval_jaxpr/ppermute | solution.py:27
  1015.5 21.0 %collective-permute-start.1 = (bf16[16,2048]{1,0:T(8,128)(2,1)S(1)}, bf16[16,2048]{1,0:T(8,128)(2,1)S(1)}, u32[]{:S(2)}, u32[]{:S(2)}) collective-permute-start(bf16[16,2048]{1,0:T(8,128)(2,1)S(1)} %get-tuple-element.1417), channel_id=1, source_target_pairs={{4,0},{8,4},{12,8},{16,12},{20,16},{24,20},{28,24},{32,28},{36,32}... | collective-permute-start | bytes 196616 | tf_op jit(solution)/shard_map/while/body/eval_jaxpr/ppermute | solution.py:27
  1064.8 27.5 %collective-permute-start.1 = (bf16[16,2048]{1,0:T(8,128)(2,1)S(1)}, bf16[16,2048]{1,0:T(8,128)(2,1)S(1)}, u32[]{:S(2)}, u32[]{:S(2)}) collective-permute-start(bf16[16,2048]{1,0:T(8,128)(2,1)S(1)} %get-tuple-element.1417), channel_id=1, source_target_pairs={{4,0},{8,4},{12,8},{16,12},{20,16},{24,20},{28,24},{32,28},{36,32}... | collective-permute-start | bytes 196616 | tf_op jit(solution)/shard_map/while/body/eval_jaxpr/ppermute | solution.py:27
  1120.5 21.3 %collective-permute-start.1 = (bf16[16,2048]{1,0:T(8,128)(2,1)S(1)}, bf16[16,2048]{1,0:T(8,128)(2,1)S(1)}, u32[]{:S(2)}, u32[]{:S(2)}) collective-permute-start(bf16[16,2048]{1,0:T(8,128)(2,1)S(1)} %get-tuple-element.1417), channel_id=1, source_target_pairs={{4,0},{8,4},{12,8},{16,12},{20,16},{24,20},{28,24},{32,28},{36,32}... | collective-permute-start | bytes 196616 | tf_op jit(solution)/shard_map/while/body/eval_jaxpr/ppermute | solution.py:27
  1170.0 21.2 %collective-permute-start.1 = (bf16[16,2048]{1,0:T(8,128)(2,1)S(1)}, bf16[16,2048]{1,0:T(8,128)(2,1)S(1)}, u32[]{:S(2)}, u32[]{:S(2)}) collective-permute-start(bf16[16,2048]{1,0:T(8,128)(2,1)S(1)} %get-tuple-element.1417), channel_id=1, source_target_pairs={{4,0},{8,4},{12,8},{16,12},{20,16},{24,20},{28,24},{32,28},{36,32}... | collective-permute-start | bytes 196616 | tf_op jit(solution)/shard_map/while/body/eval_jaxpr/ppermute | solution.py:27
  1219.4 21.2 %collective-permute-start.1 = (bf16[16,2048]{1,0:T(8,128)(2,1)S(1)}, bf16[16,2048]{1,0:T(8,128)(2,1)S(1)}, u32[]{:S(2)}, u32[]{:S(2)}) collective-permute-start(bf16[16,2048]{1,0:T(8,128)(2,1)S(1)} %get-tuple-element.1417), channel_id=1, source_target_pairs={{4,0},{8,4},{12,8},{16,12},{20,16},{24,20},{28,24},{32,28},{36,32}... | collective-permute-start | bytes 196616 | tf_op jit(solution)/shard_map/while/body/eval_jaxpr/ppermute | solution.py:27
  1268.7 21.1 %collective-permute-start.1 = (bf16[16,2048]{1,0:T(8,128)(2,1)S(1)}, bf16[16,2048]{1,0:T(8,128)(2,1)S(1)}, u32[]{:S(2)}, u32[]{:S(2)}) collective-permute-start(bf16[16,2048]{1,0:T(8,128)(2,1)S(1)} %get-tuple-element.1417), channel_id=1, source_target_pairs={{4,0},{8,4},{12,8},{16,12},{20,16},{24,20},{28,24},{32,28},{36,32}... | collective-permute-start | bytes 196616 | tf_op jit(solution)/shard_map/while/body/eval_jaxpr/ppermute | solution.py:27
  1322.3 8.5 collective-permute-start.1
  (54 other events, 1700.2 us)
Sparse Core Ops, SparseCore 0:
  24.9 26.1 all-gather.1
where the time goes:
time: 1620 us; the launch traced here: 1610 us
  blocking collectives  894 us (55%)
  waiting for transfers between devices  355 us (22%)
  starting transfers between devices  116 us (7%)
  matrix products  92 us (6%)
  other arithmetic  65.3 us (4%)
  local copies, waits for them, and re-layouts  56.8 us (4%)
    all_gather x35, blocking collectives, one_step(): lax.all_gather(backward_piece, 'pt', axis=1, tiled=True)  420 us
    all_gather x35, blocking collectives, one_step(): lax.all_gather(forward_piece, 'pt', axis=1, tiled=True)  419 us
    ppermute x70, waiting for transfers between devices, shifted(): return lax.ppermute(block, axis, route)  355 us
    ppermute x70, starting transfers between devices, shifted(): return lax.ppermute(block, axis, route)  111 us
    another operation x66, local copies, waits for them, and re-layouts  40.7 us
    dot_general x32, matrix products, squared_dist(): lax.dot_general(left_pts, right_pts, (((0,), (0,)), ((), ())), preferred_...  39 us
  transfers between devices with their start and end apart: 73, of which 35 were waited for; matrix products, arithmetic and copies ran while one was open for 8% of the time, Pallas kernels for 0%

commit v1 on v0

--- a/solution.py
+++ b/solution.py
@@ -2,6 +2,18 @@
 import jax.numpy as jnp
 from jax import lax
 from jax.sharding import PartitionSpec as P
+
+
+def collect(array, axis, dim):
+    ways, here, step = (lax.axis_size(axis), lax.axis_index(axis), array.shape[dim])
+    line, have = (array, 1)
+    while have < ways:
+        line = jnp.concatenate(
+            [line, lax.ppermute(line, axis, [(d, (d - have) % ways) for d in range(ways)])],
+            axis=dim,
+        )
+        have = 2 * have
+    return jnp.roll(line, here * step, axis=dim)
 
 
 def with_halo(cells, sides, width):
@@ -122,7 +134,7 @@
         backward_piece = jnp.where(day_index == day_count - 1, seed_rows, backward_got)
         forward_full, backward_full = (
             lax.all_gather(forward_piece, "pt", axis=1, tiled=True),
-            lax.all_gather(backward_piece, "pt", axis=1, tiled=True),
+            collect(backward_piece, "pt", 1),
         )
         forward_own, forward_all = settle(forward_piece, forward_full, forward_ok)
         backward_own, backward_all = settle(backward_piece, backward_full, backward_ok)

time: 1620 us -> 1440 us (0.89)
  blocking collectives: 894 us -> 476 us
  waiting for transfers between devices: 355 us -> 495 us
  starting transfers between devices: 116 us -> 220 us
    all_gather x35 -> x0, blocking collectives: 420 us -> none  [one_step(): lax.all_gather(backward_piece, 'pt', axis=1, tiled=True)]
    ppermute x0 -> x70, waiting for transfers between devices: none -> 152 us  [collect(): lax.ppermute(line, axis, [(d, (d - have) % ways) for d in range(ways)])]
    ppermute x0 -> x70, starting transfers between devices: none -> 93.1 us  [collect(): lax.ppermute(line, axis, [(d, (d - have) % ways) for d in range(ways)])]
    while x0 -> x35, other arithmetic: none -> 26.9 us
    select_n x35 -> x0, other arithmetic: 26.9 us -> none  [one_step(): jnp.where(day_index == day_count - 1, seed_rows, backward_got)]
  transfers between devices with their start and end apart: 73 -> 143, of which waited for: 35 -> 70; matrix products, arithmetic and copies ran while one was open for 8% -> 9% of each run, Pallas kernels for 0% -> 0%
where the time goes in v1:
time: 1440 us
  waiting for transfers between devices  495 us (34%)
  blocking collectives  476 us (33%)
  starting transfers between devices  220 us (15%)
  matrix products  92 us (6%)
  other arithmetic  65.6 us (5%)
  local copies, waits for them, and re-layouts  57.7 us (4%)
  between operations  15.5 us (1%)
  loops' own time  14.6 us (1%)
    all_gather x35, blocking collectives, one_step(): lax.all_gather(forward_piece, 'pt', axis=1, tiled=True)  423 us
    ppermute x70, waiting for transfers between devices, shifted(): return lax.ppermute(block, axis, route)  343 us
    ppermute x70, waiting for transfers between devices, collect(): lax.ppermute(line, axis, [(d, (d - have) % ways) for d in range(ways)])  152 us
    ppermute x70, starting transfers between devices, shifted(): return lax.ppermute(block, axis, route)  123 us
    ppermute x70, starting transfers between devices, collect(): lax.ppermute(line, axis, [(d, (d - have) % ways) for d in range(ways)])  93.1 us
    another operation x66, local copies, waits for them, and re-layouts  40.7 us
    dot_general x32, matrix products, squared_dist(): lax.dot_general(left_pts, right_pts, (((0,), (0,)), ((), ())), preferred_...  39 us
  transfers between devices with their start and end apart: 143, of which 70 were waited for; matrix products, arithmetic and copies ran while one was open for 9% of the time, Pallas kernels for 0%

profile of v1, /device:TPU:0, one launch (start us, length us, event | category | flops | bytes accessed | tf_op | source)
XLA Modules:
  0.0 1436.1 jit_solution(11165994091460561351)
XLA Ops:
  7.2 13.1 all_gather.22
  24.8 13.6 all_gather.23
  50.4 1268.4 %while.77 = (s32[]{:T(128)}, bf16[16,2048]{1,0:T(8,128)(2,1)S(1)}, bf16[16,2048]{1,0:T(8,128)(2,1)S(1)}, f32[64,512]{1,0:T(8,128)S(1)}, f32[64,512]{1,0:T(8,128)...) while((s32[]{:T(128)}, bf16[16,2048]{1,0:T(8,128)(2,1)S(1)}, ...), condition=%wide.region_14.15_spmd.clone.clone, body=%wide.region_3.14_spmd.clone.clone.sunk | while | flops 87101472 | bytes 3426280 | solution.py:169
  222.4 12.1 all_gather.29
  258.5 12.1 all_gather.29
  288.2 12.1 all_gather.29
  318.0 12.1 all_gather.29
  350.9 12.1 all_gather.29
  381.2 12.1 all_gather.29
  527.7 13.2 collective-permute-done.3
  723.8 16.3 %collective-permute-done.3 = bf16[16,2048]{1,0:T(8,128)(2,1)S(1)} collective-permute-done((bf16[16,2048]{1,0:T(8,128)(2,1)S(1)}, bf16[16,2048]{1,0:T(8,128)(2,1)S(1)}, u32[]{:S(2)}, u32[]{:S(2)}) %collective-permute-start.3) | collective-permute-done | bytes 65568 | tf_op jit(solution)/shard_map/while/body/eval_jaxpr/ppermute | solution.py:39
  764.2 12.9 collective-permute-done.3
  802.5 17.8 %collective-permute-done.3 = bf16[16,2048]{1,0:T(8,128)(2,1)S(1)} collective-permute-done((bf16[16,2048]{1,0:T(8,128)(2,1)S(1)}, bf16[16,2048]{1,0:T(8,128)(2,1)S(1)}, u32[]{:S(2)}, u32[]{:S(2)}) %collective-permute-start.3) | collective-permute-done | bytes 65568 | tf_op jit(solution)/shard_map/while/body/eval_jaxpr/ppermute | solution.py:39
  844.3 26.4 %collective-permute-done.3 = bf16[16,2048]{1,0:T(8,128)(2,1)S(1)} collective-permute-done((bf16[16,2048]{1,0:T(8,128)(2,1)S(1)}, bf16[16,2048]{1,0:T(8,128)(2,1)S(1)}, u32[]{:S(2)}, u32[]{:S(2)}) %collective-permute-start.3) | collective-permute-done | bytes 65568 | tf_op jit(solution)/shard_map/while/body/eval_jaxpr/ppermute | solution.py:39
  896.1 20.0 %collective-permute-done.3 = bf16[16,2048]{1,0:T(8,128)(2,1)S(1)} collective-permute-done((bf16[16,2048]{1,0:T(8,128)(2,1)S(1)}, bf16[16,2048]{1,0:T(8,128)(2,1)S(1)}, u32[]{:S(2)}, u32[]{:S(2)}) %collective-permute-start.3) | collective-permute-done | bytes 65568 | tf_op jit(solution)/shard_map/while/body/eval_jaxpr/ppermute | solution.py:39
  940.6 25.9 %collective-permute-done.3 = bf16[16,2048]{1,0:T(8,128)(2,1)S(1)} collective-permute-done((bf16[16,2048]{1,0:T(8,128)(2,1)S(1)}, bf16[16,2048]{1,0:T(8,128)(2,1)S(1)}, u32[]{:S(2)}, u32[]{:S(2)}) %collective-permute-start.3) | collective-permute-done | bytes 65568 | tf_op jit(solution)/shard_map/while/body/eval_jaxpr/ppermute | solution.py:39
  991.9 20.0 %collective-permute-done.3 = bf16[16,2048]{1,0:T(8,128)(2,1)S(1)} collective-permute-done((bf16[16,2048]{1,0:T(8,128)(2,1)S(1)}, bf16[16,2048]{1,0:T(8,128)(2,1)S(1)}, u32[]{:S(2)}, u32[]{:S(2)}) %collective-permute-start.3) | collective-permute-done | bytes 65568 | tf_op jit(solution)/shard_map/while/body/eval_jaxpr/ppermute | solution.py:39
  1035.6 19.8 %collective-permute-done.3 = bf16[16,2048]{1,0:T(8,128)(2,1)S(1)} collective-permute-done((bf16[16,2048]{1,0:T(8,128)(2,1)S(1)}, bf16[16,2048]{1,0:T(8,128)(2,1)S(1)}, u32[]{:S(2)}, u32[]{:S(2)}) %collective-permute-start.3) | collective-permute-done | bytes 65568 | tf_op jit(solution)/shard_map/while/body/eval_jaxpr/ppermute | solution.py:39
  1081.6 18.8 %collective-permute-done.3 = bf16[16,2048]{1,0:T(8,128)(2,1)S(1)} collective-permute-done((bf16[16,2048]{1,0:T(8,128)(2,1)S(1)}, bf16[16,2048]{1,0:T(8,128)(2,1)S(1)}, u32[]{:S(2)}, u32[]{:S(2)}) %collective-permute-start.3) | collective-permute-done | bytes 65568 | tf_op jit(solution)/shard_map/while/body/eval_jaxpr/ppermute | solution.py:39
  1103.6 12.2 all_gather.29
  1127.8 16.5 %collective-permute-done.3 = bf16[16,2048]{1,0:T(8,128)(2,1)S(1)} collective-permute-done((bf16[16,2048]{1,0:T(8,128)(2,1)S(1)}, bf16[16,2048]{1,0:T(8,128)(2,1)S(1)}, u32[]{:S(2)}, u32[]{:S(2)}) %collective-permute-start.3) | collective-permute-done | bytes 65568 | tf_op jit(solution)/shard_map/while/body/eval_jaxpr/ppermute | solution.py:39
  1321.0 52.7 %while.75 = (s32[]{:T(128)}, f32[16,512]{1,0:T(8,128)S(1)}, f32[512]{0:T(512)S(1)}, s32[16]{0:T(128)S(1)}, f32[8192]{0:T(1024)S(1)}, /*index=5*/bf16[64,8192]{1,...) while((s32[]{:T(128)}, f32[16,512]{1,0:T(8,128)S(1)}, ...), condition=%wide.region_20.21_spmd, body=%wide.region_19.20_spmd.sunk | while | flops 37748740 | bytes 2244795 | solution.py:192
  1373.7 15.6 %all-reduce = (f32[8192]{0:T(1024)S(1)}, f32[]{:T(128)}) all-reduce(f32[8192]{0:T(1024)S(1)} %bitcast.96, f32[]{:T(128)} %get-tuple-element.1170), channel_id=1, replica_groups=mesh['day'=32,'pt'=4] {'pt'}, use_global_device_ids=true, to_apply=%region_21.22 | all-reduce | flops 8193 | bytes 65544 | tf_op jit(solution)/shard_map/psum | solution.py:193
  1390.0 38.6 %while.76 = (s32[]{:T(128)}, f32[512]{0:T(512)S(1)}, f32[512]{0:T(512)S(1)}, f32[8192]{0:T(1024)S(1)}, bf16[64,8192]{1,0:T(8,128)(2,1)}, /*index=5*/bf16[64,512]...) while((s32[]{:T(128)}, f32[512]{0:T(512)S(1)}, ...), condition=%wide.region_23.24_spmd.clone, body=%wide.region_22.23_spmd.clone.sunk | while | flops 37749764 | bytes 2250929 | solution.py:204
  (1089 shorter events, 1168.2 us)
Async XLA Ops:
  7.2 1312.3 %all-gather.2.cloned.1.call-start = ((), (), s32[]{:S(2)}) async-start(), calls=%async_computation | async-start | bytes 1310720 | tf_op jit(solution)/shard_map/all_gather | solution.py:177
  20.3 29.9 %collective-permute-start.5 = (bf16[1,64,2048]{2,1,0:T(8,128)(2,1)S(1)}, bf16[1,64,2048]{2,1,0:T(8,128)(2,1)S(1)}, u32[]{:S(2)}, u32[]{:S(2)}) collective-permute-start(bf16[1,64,2048]{2,1,0:T(8,128)(2,1)S(1)} %all_gather.22), channel_id=1, source_target_pairs={{4,0},{8,4},{12,8},{16,12},{20,16},{24,20},{28,24},{32,28},{36,32}... | collective-permute-start | bytes 786440 | tf_op jit(solution)/shard_map/ppermute | solution.py:29
  21.7 28.6 %collective-permute-start.4 = (bf16[1,64,2048]{2,1,0:T(8,128)(2,1)S(1)}, bf16[1,64,2048]{2,1,0:T(8,128)(2,1)S(1)}, u32[]{:S(2)}, u32[]{:S(2)}) collective-permute-start(bf16[1,64,2048]{2,1,0:T(8,128)(2,1)S(1)} %all_gather.22), channel_id=1, source_target_pairs={{0,4},{4,8},{8,12},{12,16},{16,20},{20,24},{24,28},{28,32},{32,36}... | collective-permute-start | bytes 786440 | tf_op jit(solution)/shard_map/ppermute | solution.py:27
  52.5 15.0 %collective-permute-start = (f32[16,512]{1,0:T(8,128)S(1)}, f32[16,512]{1,0:T(8,128)S(1)}, u32[]{:S(2)}, u32[]{:S(2)}) collective-permute-start(f32[16,512]{1,0:T(8,128)S(1)} %get-tuple-element.1482), channel_id=1, source_target_pairs={{0,3},{1,0},{2,1},{3,2},{4,7},{5,4},{6,5},{7,6},{8,11},{9,8},{10,9... | collective-permute-start | bytes 98312 | tf_op jit(solution)/shard_map/while/body/eval_jaxpr/ppermute | solution.py:12
  526.3 14.6 %collective-permute-start.3 = (bf16[16,2048]{1,0:T(8,128)(2,1)S(1)}, bf16[16,2048]{1,0:T(8,128)(2,1)S(1)}, u32[]{:S(2)}, u32[]{:S(2)}) collective-permute-start(bf16[16,2048]{1,0:T(8,128)(2,1)S(1)} %get-tuple-element.1489), channel_id=1, source_target_pairs={{4,0},{8,4},{12,8},{16,12},{20,16},{24,20},{28,24},{32,28},{36,32}... | collective-permute-start | bytes 196616 | tf_op jit(solution)/shard_map/while/body/eval_jaxpr/ppermute | solution.py:39
  606.2 14.6 %collective-permute-start = (f32[16,512]{1,0:T(8,128)S(1)}, f32[16,512]{1,0:T(8,128)S(1)}, u32[]{:S(2)}, u32[]{:S(2)}) collective-permute-start(f32[16,512]{1,0:T(8,128)S(1)} %get-tuple-element.1482), channel_id=1, source_target_pairs={{0,3},{1,0},{2,1},{3,2},{4,7},{5,4},{6,5},{7,6},{8,11},{9,8},{10,9... | collective-permute-start | bytes 98312 | tf_op jit(solution)/shard_map/while/body/eval_jaxpr/ppermute | solution.py:12
  669.7 14.5 %collective-permute-start = (f32[16,512]{1,0:T(8,128)S(1)}, f32[16,512]{1,0:T(8,128)S(1)}, u32[]{:S(2)}, u32[]{:S(2)}) collective-permute-start(f32[16,512]{1,0:T(8,128)S(1)} %get-tuple-element.1482), channel_id=1, source_target_pairs={{0,3},{1,0},{2,1},{3,2},{4,7},{5,4},{6,5},{7,6},{8,11},{9,8},{10,9... | collective-permute-start | bytes 98312 | tf_op jit(solution)/shard_map/while/body/eval_jaxpr/ppermute | solution.py:12
  722.4 17.7 %collective-permute-start.3 = (bf16[16,2048]{1,0:T(8,128)(2,1)S(1)}, bf16[16,2048]{1,0:T(8,128)(2,1)S(1)}, u32[]{:S(2)}, u32[]{:S(2)}) collective-permute-start(bf16[16,2048]{1,0:T(8,128)(2,1)S(1)} %get-tuple-element.1489), channel_id=1, source_target_pairs={{4,0},{8,4},{12,8},{16,12},{20,16},{24,20},{28,24},{32,28},{36,32}... | collective-permute-start | bytes 196616 | tf_op jit(solution)/shard_map/while/body/eval_jaxpr/ppermute | solution.py:39
  762.8 14.3 collective-permute-start.3
  779.1 14.5 %collective-permute-start = (f32[16,512]{1,0:T(8,128)S(1)}, f32[16,512]{1,0:T(8,128)S(1)}, u32[]{:S(2)}, u32[]{:S(2)}) collective-permute-start(f32[16,512]{1,0:T(8,128)S(1)} %get-tuple-element.1482), channel_id=1, source_target_pairs={{0,3},{1,0},{2,1},{3,2},{4,7},{5,4},{6,5},{7,6},{8,11},{9,8},{10,9... | collective-permute-start | bytes 98312 | tf_op jit(solution)/shard_map/while/body/eval_jaxpr/ppermute | solution.py:12
  801.1 19.2 %collective-permute-start.3 = (bf16[16,2048]{1,0:T(8,128)(2,1)S(1)}, bf16[16,2048]{1,0:T(8,128)(2,1)S(1)}, u32[]{:S(2)}, u32[]{:S(2)}) collective-permute-start(bf16[16,2048]{1,0:T(8,128)(2,1)S(1)} %get-tuple-element.1489), channel_id=1, source_target_pairs={{4,0},{8,4},{12,8},{16,12},{20,16},{24,20},{28,24},{32,28},{36,32}... | collective-permute-start | bytes 196616 | tf_op jit(solution)/shard_map/while/body/eval_jaxpr/ppermute | solution.py:39
  842.9 27.8 %collective-permute-start.3 = (bf16[16,2048]{1,0:T(8,128)(2,1)S(1)}, bf16[16,2048]{1,0:T(8,128)(2,1)S(1)}, u32[]{:S(2)}, u32[]{:S(2)}) collective-permute-start(bf16[16,2048]{1,0:T(8,128)(2,1)S(1)} %get-tuple-element.1489), channel_id=1, source_target_pairs={{4,0},{8,4},{12,8},{16,12},{20,16},{24,20},{28,24},{32,28},{36,32}... | collective-permute-start | bytes 196616 | tf_op jit(solution)/shard_map/while/body/eval_jaxpr/ppermute | solution.py:39
  872.7 14.6 %collective-permute-start = (f32[16,512]{1,0:T(8,128)S(1)}, f32[16,512]{1,0:T(8,128)S(1)}, u32[]{:S(2)}, u32[]{:S(2)}) collective-permute-start(f32[16,512]{1,0:T(8,128)S(1)} %get-tuple-element.1482), channel_id=1, source_target_pairs={{0,3},{1,0},{2,1},{3,2},{4,7},{5,4},{6,5},{7,6},{8,11},{9,8},{10,9... | collective-permute-start | bytes 98312 | tf_op jit(solution)/shard_map/while/body/eval_jaxpr/ppermute | solution.py:12
  894.7 21.4 %collective-permute-start.3 = (bf16[16,2048]{1,0:T(8,128)(2,1)S(1)}, bf16[16,2048]{1,0:T(8,128)(2,1)S(1)}, u32[]{:S(2)}, u32[]{:S(2)}) collective-permute-start(bf16[16,2048]{1,0:T(8,128)(2,1)S(1)} %get-tuple-element.1489), channel_id=1, source_target_pairs={{4,0},{8,4},{12,8},{16,12},{20,16},{24,20},{28,24},{32,28},{36,32}... | collective-permute-start | bytes 196616 | tf_op jit(solution)/shard_map/while/body/eval_jaxpr/ppermute | solution.py:39
  939.2 27.3 %collective-permute-start.3 = (bf16[16,2048]{1,0:T(8,128)(2,1)S(1)}, bf16[16,2048]{1,0:T(8,128)(2,1)S(1)}, u32[]{:S(2)}, u32[]{:S(2)}) collective-permute-start(bf16[16,2048]{1,0:T(8,128)(2,1)S(1)} %get-tuple-element.1489), channel_id=1, source_target_pairs={{4,0},{8,4},{12,8},{16,12},{20,16},{24,20},{28,24},{32,28},{36,32}... | collective-permute-start | bytes 196616 | tf_op jit(solution)/shard_map/while/body/eval_jaxpr/ppermute | solution.py:39
  968.5 14.6 %collective-permute-start = (f32[16,512]{1,0:T(8,128)S(1)}, f32[16,512]{1,0:T(8,128)S(1)}, u32[]{:S(2)}, u32[]{:S(2)}) collective-permute-start(f32[16,512]{1,0:T(8,128)S(1)} %get-tuple-element.1482), channel_id=1, source_target_pairs={{0,3},{1,0},{2,1},{3,2},{4,7},{5,4},{6,5},{7,6},{8,11},{9,8},{10,9... | collective-permute-start | bytes 98312 | tf_op jit(solution)/shard_map/while/body/eval_jaxpr/ppermute | solution.py:12
  990.5 21.4 %collective-permute-start.3 = (bf16[16,2048]{1,0:T(8,128)(2,1)S(1)}, bf16[16,2048]{1,0:T(8,128)(2,1)S(1)}, u32[]{:S(2)}, u32[]{:S(2)}) collective-permute-start(bf16[16,2048]{1,0:T(8,128)(2,1)S(1)} %get-tuple-element.1489), channel_id=1, source_target_pairs={{4,0},{8,4},{12,8},{16,12},{20,16},{24,20},{28,24},{32,28},{36,32}... | collective-permute-start | bytes 196616 | tf_op jit(solution)/shard_map/while/body/eval_jaxpr/ppermute | solution.py:39
  1034.2 21.2 %collective-permute-start.3 = (bf16[16,2048]{1,0:T(8,128)(2,1)S(1)}, bf16[16,2048]{1,0:T(8,128)(2,1)S(1)}, u32[]{:S(2)}, u32[]{:S(2)}) collective-permute-start(bf16[16,2048]{1,0:T(8,128)(2,1)S(1)} %get-tuple-element.1489), channel_id=1, source_target_pairs={{4,0},{8,4},{12,8},{16,12},{20,16},{24,20},{28,24},{32,28},{36,32}... | collective-permute-start | bytes 196616 | tf_op jit(solution)/shard_map/while/body/eval_jaxpr/ppermute | solution.py:39
  1057.4 14.4 %collective-permute-start = (f32[16,512]{1,0:T(8,128)S(1)}, f32[16,512]{1,0:T(8,128)S(1)}, u32[]{:S(2)}, u32[]{:S(2)}) collective-permute-start(f32[16,512]{1,0:T(8,128)S(1)} %get-tuple-element.1482), channel_id=1, source_target_pairs={{0,3},{1,0},{2,1},{3,2},{4,7},{5,4},{6,5},{7,6},{8,11},{9,8},{10,9... | collective-permute-start | bytes 98312 | tf_op jit(solution)/shard_map/while/body/eval_jaxpr/ppermute | solution.py:12
  1080.2 20.2 %collective-permute-start.3 = (bf16[16,2048]{1,0:T(8,128)(2,1)S(1)}, bf16[16,2048]{1,0:T(8,128)(2,1)S(1)}, u32[]{:S(2)}, u32[]{:S(2)}) collective-permute-start(bf16[16,2048]{1,0:T(8,128)(2,1)S(1)} %get-tuple-element.1489), channel_id=1, source_target_pairs={{4,0},{8,4},{12,8},{16,12},{20,16},{24,20},{28,24},{32,28},{36,32}... | collective-permute-start | bytes 196616 | tf_op jit(solution)/shard_map/while/body/eval_jaxpr/ppermute | solution.py:39
  1126.4 17.9 %collective-permute-start.3 = (bf16[16,2048]{1,0:T(8,128)(2,1)S(1)}, bf16[16,2048]{1,0:T(8,128)(2,1)S(1)}, u32[]{:S(2)}, u32[]{:S(2)}) collective-permute-start(bf16[16,2048]{1,0:T(8,128)(2,1)S(1)} %get-tuple-element.1489), channel_id=1, source_target_pairs={{4,0},{8,4},{12,8},{16,12},{20,16},{24,20},{28,24},{32,28},{36,32}... | collective-permute-start | bytes 196616 | tf_op jit(solution)/shard_map/while/body/eval_jaxpr/ppermute | solution.py:39
  1146.3 14.4 %collective-permute-start = (f32[16,512]{1,0:T(8,128)S(1)}, f32[16,512]{1,0:T(8,128)S(1)}, u32[]{:S(2)}, u32[]{:S(2)}) collective-permute-start(f32[16,512]{1,0:T(8,128)S(1)} %get-tuple-element.1482), channel_id=1, source_target_pairs={{0,3},{1,0},{2,1},{3,2},{4,7},{5,4},{6,5},{7,6},{8,11},{9,8},{10,9... | collective-permute-start | bytes 98312 | tf_op jit(solution)/shard_map/while/body/eval_jaxpr/ppermute | solution.py:12
  1224.8 14.6 %collective-permute-start = (f32[16,512]{1,0:T(8,128)S(1)}, f32[16,512]{1,0:T(8,128)S(1)}, u32[]{:S(2)}, u32[]{:S(2)}) collective-permute-start(f32[16,512]{1,0:T(8,128)S(1)} %get-tuple-element.1482), channel_id=1, source_target_pairs={{0,3},{1,0},{2,1},{3,2},{4,7},{5,4},{6,5},{7,6},{8,11},{9,8},{10,9... | collective-permute-start | bytes 98312 | tf_op jit(solution)/shard_map/while/body/eval_jaxpr/ppermute | solution.py:12
  1293.5 14.7 %collective-permute-start = (f32[16,512]{1,0:T(8,128)S(1)}, f32[16,512]{1,0:T(8,128)S(1)}, u32[]{:S(2)}, u32[]{:S(2)}) collective-permute-start(f32[16,512]{1,0:T(8,128)S(1)} %get-tuple-element.1482), channel_id=1, source_target_pairs={{0,3},{1,0},{2,1},{3,2},{4,7},{5,4},{6,5},{7,6},{8,11},{9,8},{10,9... | collective-permute-start | bytes 98312 | tf_op jit(solution)/shard_map/while/body/eval_jaxpr/ppermute | solution.py:12
  (124 other events, 2174.6 us)
Sparse Core Ops, SparseCore 0:
  24.9 26.1 all-gather.1
